TPU v7x, 512 devices: a whole 4x8x8 slice. The times are simulated.
512 devices in a mesh: clip: 32 (over x, y), seq: 16 (over z, core).
Axes of the slice: x: 4, y: 8, z: 8, core: 2. Of those that a mesh axis runs over, the one named last changes fastest.
Arguments:
- queries: bfloat16 [32, 2048, 4096], P('clip', 'seq'), may hold values from -34 to 34
- keys: bfloat16 [32, 2048, 4096], P('clip', 'seq'), may hold values from -6 to 6
- values: bfloat16 [32, 2048, 4096], P('clip', 'seq'), may hold values from -6 to 6
- frame_counts: int32 [128], P('clip'), may hold values from 1 to 4
- assignment: int32 [32], P('clip'), may hold values from 0 to 127
- timesteps: int32 [32], P('clip'), may hold values from 0 to 999
- gate_gain: float32 [4096], replicated, may hold values from -3 to 3
Outputs:
- attended: bfloat16 [32, 2048, 4096], P('clip', 'seq')
All inputs are finite; a program needn't handle non-finite values.
Results may differ from a plain program's by a relative error of at most 0.0086.
Values may be sent and summed in bfloat16 or wider, within the bound.
A program may use at most 128 MiB of HBM per device.

v0:
```python
import jax
import jax.numpy as jnp
from jax import lax
from jax.sharding import Mesh
from jax.sharding import PartitionSpec as P

HD = 128
FRAME_TOK = 448
GRID_W = 28
CLIP = ("clip_0", "clip_1")


def in_order(tiles, dim):
    dims = list(tiles.shape[1:])
    dims[dim] *= tiles.shape[0]
    return jnp.moveaxis(tiles, 0, dim).reshape(dims)


def all_blocks(shard, axes, sequence):
    tiles = shard
    for k in sequence:
        tiles = lax.all_gather(tiles, axes[k])
    done = sequence[::-1]
    back = [done.index(k) for k in range(len(axes))]
    tiles = tiles.transpose(*back, *range(len(axes), tiles.ndim))
    return tiles.reshape(-1, *shard.shape)


def gathered_by_axis(shard, axes, sequence, dim):
    return in_order(all_blocks(shard, axes, sequence), dim)


def sent_together(arrays, axis, split_dim, concat_dim, along):
    both = jnp.concatenate(arrays, axis=along)
    out, at, done = (
        lax.all_to_all(both, axis, split_axis=split_dim, concat_axis=concat_dim, tiled=True),
        0,
        [],
    )
    for a in arrays:
        done.append(lax.slice_in_dim(out, at, at + a.shape[along], axis=along))
        at += a.shape[along]
    return tuple(done)


def rope_tables(count):
    position = jnp.arange(count, dtype=jnp.int32)
    frame = (position // FRAME_TOK).astype(jnp.float32)
    within = position % FRAME_TOK
    row_pos = (within // GRID_W).astype(jnp.float32)
    col_pos = (within % GRID_W).astype(jnp.float32)
    temporal = jnp.arange(22, dtype=jnp.float32)
    spatial = jnp.arange(21, dtype=jnp.float32)
    inv_time = 10000.0 ** (-2.0 * temporal / 44.0)
    inv_space = 10000.0 ** (-2.0 * spatial / 42.0)
    angles = jnp.concatenate(
        [
            frame[:, None] * inv_time[None, :],
            row_pos[:, None] * inv_space[None, :],
            col_pos[:, None] * inv_space[None, :],
        ],
        axis=1,
    )
    return (jnp.cos(angles), jnp.sin(angles))


def rotate(vectors, cosine, sine):
    half = vectors.shape[-1] // 2
    first = vectors[..., :half].astype(jnp.float32)
    second = vectors[..., half:].astype(jnp.float32)
    cos_b = cosine[:, None, :]
    sin_b = sine[:, None, :]
    return jnp.concatenate(
        [first * cos_b - second * sin_b, first * sin_b + second * cos_b], axis=-1
    ).astype(jnp.bfloat16)


def masked_scores(q_block, key_rot, width, length, scale):
    scores = (
        jnp.einsum("qhd,khd->hqk", q_block, key_rot, preferred_element_type=jnp.float32) * scale
    )
    key_pos = jnp.arange(width, dtype=jnp.int32)
    return jnp.where(key_pos[None, None, :] < length, scores, -jnp.inf)


def attend(query_rot, key_rot, value, length):
    count = query_rot.shape[0]
    width = min(512, count)
    scale = HD ** (-0.5)
    results = []
    for start in range(0, count, width):
        q_block = query_rot[start : start + width]
        scores = masked_scores(q_block, key_rot, count, length, scale)
        top = jnp.max(scores, axis=-1, keepdims=True)
        weights = jnp.exp(scores - top)
        total = jnp.sum(weights, axis=-1)
        mixed = jnp.einsum(
            "hqk,khd->qhd", weights.astype(jnp.bfloat16), value, preferred_element_type=jnp.float32
        )
        results.append(mixed / jnp.transpose(total)[:, :, None])
    return jnp.concatenate(results, axis=0).astype(jnp.bfloat16)


def local(queries, keys, values, frame_counts, assignment, timesteps, gate_gain):
    counts_all = gathered_by_axis(frame_counts, CLIP, (0, 1), 0)
    slots = jnp.arange(counts_all.shape[0], dtype=jnp.int32)
    picked = jnp.sum(jnp.where(slots == assignment[0], counts_all, 0))
    length = picked * FRAME_TOK
    fraction = timesteps[0].astype(jnp.float32) / 1000.0
    sigma = 5.0 * fraction / (1.0 + 4.0 * fraction)
    tok_rows = queries.shape[1]
    feature_count = queries.shape[2]
    groups = lax.axis_size("seq")
    heads_local = feature_count // HD // groups
    query_rows = queries.reshape(tok_rows, groups, heads_local, HD)
    key_rows = keys.reshape(tok_rows, groups, heads_local, HD)
    value_rows = values.reshape(tok_rows, groups, heads_local, HD)
    q_heads, k_heads, v_heads = sent_together((query_rows, key_rows, value_rows), "seq", 1, 0, 2)
    count = q_heads.shape[0]
    heads_here = q_heads.shape[2]
    cosine, sine = rope_tables(count)
    query_rot = rotate(q_heads.reshape(count, heads_here, HD), cosine, sine)
    key_rot = rotate(k_heads.reshape(count, heads_here, HD), cosine, sine)
    mixed = attend(query_rot, key_rot, v_heads.reshape(count, heads_here, HD), length)
    mixed = mixed.reshape(count, 1, heads_here, HD)
    returned = lax.all_to_all(mixed, "seq", split_axis=0, concat_axis=1, tiled=True)
    returned = returned.reshape(tok_rows, feature_count).astype(jnp.float32)
    position = lax.axis_index("seq") * tok_rows + jnp.arange(tok_rows, dtype=jnp.int32)
    gated = returned * (1.0 + sigma * gate_gain[None, :])
    attended = jnp.where(position[:, None] < length, gated, 0.0).astype(jnp.bfloat16)
    return attended[None]


def solution(mesh):
    finer = Mesh(mesh.devices.reshape(4, 8, mesh.shape["seq"]), ("clip_0", "clip_1", "seq"))
    in_specs = (
        P(CLIP, "seq", None),
        P(CLIP, "seq", None),
        P(CLIP, "seq", None),
        P(CLIP),
        P(CLIP),
        P(CLIP),
        P(),
    )
    out_specs = P(CLIP, "seq", None)
    return jax.shard_map(local, mesh=finer, in_specs=in_specs, out_specs=out_specs, check_vma=False)
```

profile of v0, /device:TPU:1, one launch (start us, length us, event | category | flops | bytes accessed | tf_op | source)
XLA Modules:
  0.0 183.7 jit_solution(16581078526620594948)
XLA Ops:
  0.0 2.3 %copy.23 = bf16[1,128,4096]{1,2,0:T(8,128)(2,1)} copy(bf16[1,128,4096]{2,1,0:T(8,128)(2,1)} %param.7) | data formatting | bytes 2097152 | tf_op args[0]
  2.3 2.3 %copy.24 = bf16[1,128,4096]{1,2,0:T(8,128)(2,1)} copy(bf16[1,128,4096]{2,1,0:T(8,128)(2,1)} %param.8) | data formatting | bytes 2097152 | tf_op args[1]
  4.6 2.3 %copy.25 = bf16[1,128,4096]{1,2,0:T(8,128)(2,1)} copy(bf16[1,128,4096]{2,1,0:T(8,128)(2,1)} %param.9) | data formatting | bytes 2097152 | tf_op args[2]
  6.8 0.0 copy-start.9
  6.8 2.0 %pad_maximum_fusion = bf16[128,16,6,128]{0,3,2,1:T(8,128)(2,1)S(1)} fusion(bf16[128,16,2,128]{0,3,2,1:T(8,128)(2,1)} %bitcast.88, bf16[128,16,2,128]{0,3,2,1:T(8,128)(2,1)} %bitcast.87, bf16[128,16,2,128]{0,3,2,1:T(8,128)(2,1)} %bitcast.86), kind=kLoop, calls=%fused_computation.28 | loop fusion | flops 3145728 | bytes 6291456 | tf_op jit(solution)/shard_map/concatenate | solution.py:34
  8.9 2.8 %copy.26 = bf16[128,16,6,128]{3,0,2,1:T(8,128)(2,1)} copy(bf16[128,16,6,128]{0,3,2,1:T(8,128)(2,1)S(1)} %pad_maximum_fusion) | data formatting | bytes 6291456 | tf_op jit(solution)/shard_map/concatenate | solution.py:34
  11.7 11.8 %all-to-all-start = ((bf16[128,16,6,128]{3,0,2,1:T(8,128)(2,1)}), bf16[128,16,6,128]{3,0,2,1:T(8,128)(2,1)S(1)}, u32[]{:S(2)}, u32[]{:S(2)}) async-start(bf16[128,16,6,128]{3,0,2,1:T(8,128)(2,1)} %copy.26), calls=%async_computation | async-start | bytes 6291456 | tf_op jit(solution)/shard_map/all_to_all | solution.py:36
  23.5 1.3 dynamic-slice
  25.4 0.0 copy-done.9
  25.4 0.2 dynamic-update-slice
  25.7 7.4 %all-reduce = s32[16]{0:T(128)S(1)} all-reduce(s32[16]{0:T(128)S(1)} %dynamic-update-slice), channel_id=2, replica_groups=mesh['clip_0'=4,'clip_1'=8,'seq'=16] {'clip_0'}, use_global_device_ids=true, to_apply=%add | all-reduce | flops 16 | bytes 128
  33.1 0.1 reshape.313
  33.9 20.1 %all-gather.2 = s32[8,4,4]{2,1,0:T(4,128)S(1)} all-gather(s32[1,4,4]{2,1,0:T(4,128)S(1)} %reshape.313), channel_id=3, replica_groups=mesh['clip_0'=4,'clip_1'=8,'seq'=16] {'clip_1'}, dimensions={0}, use_global_device_ids=true | all-gather | bytes 576 | tf_op jit(solution)/shard_map/all_gather | solution.py:22
  53.9 0.6 fusion.91
  55.2 0.3 broadcast_multiply_fusion.2
  55.5 0.6 broadcast_multiply_fusion.1
  56.1 5.2 %fusion.123 = (f32[2048,64]{1,0:T(8,128)}, f32[2048,64]{1,0:T(8,128)}) fusion(f32[2048,21]{1,0:T(8,128)S(1)} %get-tuple-element.23, f32[2048,21]{1,0:T(8,128)S(1)} %get-tuple-element.22, f32[2048,22]{1,0:T(8,128)S(1)} %broadcast_multiply_fusion.2), kind=kLoop, calls=%fused_computation.132 | loop fusion | flops 262144 | bytes 1572864 | tf_op jit(solution)/shard_map/cos | solution.py:64
  61.3 33.2 %all-to-all-done = bf16[128,16,6,128]{3,0,2,1:T(8,128)(2,1)S(1)} async-done(((bf16[128,16,6,128]{3,0,2,1:T(8,128)(2,1)}), bf16[128,16,6,128]{3,0,2,1:T(8,128)(2,1)S(1)}, u32[]{:S(2)}, u32[]{:S(2)}) %all-to-all-start) | async-done | bytes 3145760 | tf_op jit(solution)/shard_map/all_to_all | solution.py:36
  94.5 0.0 copy-start.4
  94.5 0.0 copy-start.5
  94.5 0.2 copy.27
  94.7 0.0 copy-start.2
  94.7 0.1 slice_bitcast_fusion.1
  94.9 1.0 copy-done.4
  95.9 1.1 copy-done.5
  97.0 1.8 fusion.25
  98.8 0.0 copy-start
  98.8 0.6 pad_maximum_fusion.2
  99.4 0.0 copy-done.2
  99.4 0.0 copy-start.1
  99.4 1.3 fusion.81
  100.7 1.3 fusion.89
  102.0 0.0 copy-done
  102.0 0.0 copy-done.1
  102.0 4.6 %fusion = (f32[2,512]{1,0:T(2,128)S(1)}, f32[2,512,2048]{2,1,0:T(8,128)}) fusion(pred[2048]{0:T(1024)(128)(4,1)S(1)} %iota_compare_fusion, bf16[2048,2,128]{2,0,1:T(8,128)(2,1)S(1)} %pad_maximum_fusion.2, bf16[2048,2,64]{2,0,1:T(8,128)(2,1)S(1)} %get-tuple-element.12, bf16[2048,2,64]{2,0,1:T(8,128)(2,1)S(1)} %get-tuple-element.13), kind=kOutput, calls=%fused_computation.8 | convolution fusion | flops 543685632 | bytes 10491904 | tf_op jit(solution)/shard_map/qhd,khd->hqk/dot_general | solution.py:80
  106.6 10.3 %fusion.4 = (f32[2,512]{1,0:T(2,128)}, f32[2,512]{1,0:T(2,128)}, f32[2,512]{1,0:T(2,128)}, f32[2,512]{1,0:T(2,128)S(1)}, f32[2,512,2048]{2,1,0:T(8,128)}) fusion(f32[2,512,2048]{2,1,0:T(8,128)} %get-tuple-element.25, f32[2,512]{1,0:T(2,128)S(1)} %get-tuple-element.24, pred[2048]{0:T(1024)(128)(4,1)S(1)} %iota_compare_fusion, ...), kind=kOutput, calls=%fused_computation.12 | convolution fusion | flops 564654080 | bytes 35674112 | tf_op jit(solution)/shard_map/qhd,khd->hqk/dot_general | solution.py:80
  116.9 0.0 copy-start.7
  116.9 0.0 copy-start.8
  116.9 5.7 %fusion.77 = bf16[512,1,2,128]{0,3,2,1:T(8,128)(2,1)S(1)} fusion(f32[2,512,2048]{2,1,0:T(8,128)} %get-tuple-element.25, f32[2,512]{1,0:T(2,128)S(1)} %get-tuple-element.24, pred[2048]{0:T(1024)(128)(4,1)S(1)} %iota_compare_fusion, bf16[2048,1,6,128]{3,0,2,1:T(8,128)(2,1)} %bitcast.81, f32[512,2]{0,1:T(2,128)} %bitcast.92), kind=kOutput, calls=%fused_computation.68 | convolution fusion | flops 545521664 | bytes 9709568 | tf_op jit(solution)/shard_map/hqk,khd->qhd/dot_general | solution.py:97
  122.6 0.0 copy-done.7
  122.6 0.0 copy-done.8
  122.6 0.0 copy-start.3
  122.6 7.8 %fusion.6 = (f32[2,512]{1,0:T(2,128)S(1)}, f32[2,512]{1,0:T(2,128)S(1)}, f32[2,512]{1,0:T(2,128)S(1)}) fusion(f32[2,512,2048]{2,1,0:T(8,128)} %get-tuple-element.26, f32[2,512]{1,0:T(2,128)S(1)} %copy-done.8, pred[2048]{0:T(1024)(128)(4,1)S(1)} %iota_compare_fusion, f32[2,512]{1,0:T(2,128)S(1)} %copy-done.7, f32[2,512,2048]{2,1,0:T(8,128)S(1)} %fusion.81, ...), kind=kLoop, calls=%fused_computation.14 | loop fusion | flops 25162752 | bytes 25192448 | tf_op jit(solution)/shard_map/reduce_sum | solution.py:96
  130.4 0.0 copy-done.3
  130.4 5.4 %fusion.68 = bf16[512,1,2,128]{0,3,2,1:T(8,128)(2,1)S(1)} fusion(f32[2,512,2048]{2,1,0:T(8,128)} %get-tuple-element.26, f32[2,512]{1,0:T(2,128)S(1)} %copy-done.8, pred[2048]{0:T(1024)(128)(4,1)S(1)} %iota_compare_fusion, bf16[2048,1,6,128]{3,0,2,1:T(8,128)(2,1)S(1)} %bitcast.82, f32[512,2]{0,1:T(2,128)S(1)} %bitcast.91), kind=kOutput, calls=%fused_computation.65 | convolution fusion | flops 545521664 | bytes 9709568 | tf_op jit(solution)/shard_map/hqk,khd->qhd/dot_general | solution.py:97
  135.8 2.3 %fusion.59 = bf16[512,1,2,128]{0,3,2,1:T(8,128)(2,1)S(1)} fusion(f32[2,512,2048]{2,1,0:T(8,128)S(1)} %fusion.81, f32[2,512]{1,0:T(2,128)S(1)} %copy-done.7, pred[2048]{0:T(1024)(128)(4,1)S(1)} %iota_compare_fusion, bf16[2048,1,6,128]{3,0,2,1:T(8,128)(2,1)S(1)} %bitcast.83, f32[512,2]{0,1:T(2,128)S(1)} %bitcast.90), kind=kOutput, calls=%fused_computation.62 | convolution fusion | flops 545521664 | bytes 9709568 | tf_op jit(solution)/shard_map/hqk,khd->qhd/dot_general | solution.py:97
  138.2 0.0 copy-start.6
  138.2 2.4 %fusion.50 = bf16[512,1,2,128]{0,3,2,1:T(8,128)(2,1)S(1)} fusion(f32[2,512,2048]{2,1,0:T(8,128)S(1)} %fusion.89, f32[2,512]{1,0:T(2,128)S(1)} %get-tuple-element.8, pred[2048]{0:T(1024)(128)(4,1)S(1)} %iota_compare_fusion, bf16[2048,1,6,128]{3,0,2,1:T(8,128)(2,1)S(1)} %bitcast.84, f32[512,2]{0,1:T(2,128)S(1)} %bitcast.89), kind=kOutput, calls=%fused_computation.59 | convolution fusion | flops 545521664 | bytes 9709568 | tf_op jit(solution)/shard_map/hqk,khd->qhd/dot_general | solution.py:97
  140.6 0.1 pad_maximum_fusion.3
  140.7 2.0 %copy.32 = bf16[2048,1,2,128]{3,2,1,0:T(2,128)(2,1)} copy(bf16[2048,1,2,128]{0,3,2,1:T(8,128)(2,1)S(1)} %pad_maximum_fusion.3) | data formatting | bytes 2097152 | tf_op jit(solution)/shard_map/concatenate | solution.py:101
  142.7 5.4 %all-to-all-start.1 = ((bf16[2048,1,2,128]{3,2,1,0:T(2,128)(2,1)}), bf16[2048,1,2,128]{3,2,1,0:T(2,128)(2,1)S(1)}, u32[]{:S(2)}, u32[]{:S(2)}) async-start(bf16[2048,1,2,128]{3,2,1,0:T(2,128)(2,1)} %copy.32), calls=%async_computation.1 | async-start | bytes 2097152 | tf_op jit(solution)/shard_map/all_to_all | solution.py:126
  148.9 0.0 copy-done.6
  148.9 27.2 %all-to-all-done.1 = bf16[2048,1,2,128]{3,2,1,0:T(2,128)(2,1)S(1)} async-done(((bf16[2048,1,2,128]{3,2,1,0:T(2,128)(2,1)}), bf16[2048,1,2,128]{3,2,1,0:T(2,128)(2,1)S(1)}, u32[]{:S(2)}, u32[]{:S(2)}) %all-to-all-start.1) | async-done | bytes 1048608 | tf_op jit(solution)/shard_map/all_to_all | solution.py:126
  176.1 0.9 convert_bitcast_fusion
  177.0 2.6 %copy.33 = f32[128,16,1,2,128]{4,3,1,0,2:T(2,128)} copy(f32[128,16,1,2,128]{4,3,0,1,2:T(2,128)S(1)} %convert_bitcast_fusion) | data formatting | bytes 4194304 | tf_op jit(solution)/shard_map/convert_element_type | solution.py:127
  179.5 2.9 %reshape.306 = f32[1,128,4096]{2,1,0:T(8,128)S(1)} reshape(f32[128,16,1,2,128]{4,3,1,0,2:T(2,128)} %copy.33) | data formatting | bytes 4194304 | tf_op jit(solution)/shard_map/convert_element_type | solution.py:127
  182.5 1.2 select_convert_fusion
  (8 shorter events, 0.1 us)
Async XLA Ops:
  6.8 18.6 %copy-start.9 = (s32[4]{0:T(128)S(1)}, s32[4]{0:T(128)}, u32[]{:S(2)}) copy-start(s32[4]{0:T(128)} %param.10) | copy-start | bytes 52
  11.7 82.8 %all-to-all-start = ((bf16[128,16,6,128]{3,0,2,1:T(8,128)(2,1)}), bf16[128,16,6,128]{3,0,2,1:T(8,128)(2,1)S(1)}, u32[]{:S(2)}, u32[]{:S(2)}) async-start(bf16[128,16,6,128]{3,0,2,1:T(8,128)(2,1)} %copy.26), calls=%async_computation | async-start | bytes 6291456 | tf_op jit(solution)/shard_map/all_to_all | solution.py:36
  94.5 1.4 copy-start.4
  94.5 2.5 %copy-start.5 = (f32[2048,64]{1,0:T(8,128)S(1)}, f32[2048,64]{1,0:T(8,128)}, u32[]{:S(2)}) copy-start(f32[2048,64]{1,0:T(8,128)} %get-tuple-element.19) | copy-start | bytes 1572868
  94.7 4.7 %copy-start.2 = (bf16[16,128,1,6,128]{4,1,0,3,2:T(8,128)(2,1)}, bf16[16,128,1,6,128]{4,1,0,3,2:T(8,128)(2,1)S(1)}, u32[]{:S(2)}) copy-start(bf16[16,128,1,6,128]{4,1,0,3,2:T(8,128)(2,1)S(1)} %copy.27) | copy-start | bytes 9437188
  98.8 3.2 %copy-start = (bf16[2048,2,64]{2,0,1:T(8,128)(2,1)}, bf16[2048,2,64]{2,0,1:T(8,128)(2,1)S(1)}, u32[]{:S(2)}) copy-start(bf16[2048,2,64]{2,0,1:T(8,128)(2,1)S(1)} %get-tuple-element.13) | copy-start | bytes 1572868
  99.4 2.6 %copy-start.1 = (bf16[2048,2,128]{2,0,1:T(8,128)(2,1)}, bf16[2048,2,128]{2,0,1:T(8,128)(2,1)S(1)}, u32[]{:S(2)}) copy-start(bf16[2048,2,128]{2,0,1:T(8,128)(2,1)S(1)} %pad_maximum_fusion.2) | copy-start | bytes 3145732
  116.9 5.7 %copy-start.7 = (f32[2,512]{1,0:T(2,128)S(1)}, f32[2,512]{1,0:T(2,128)}, u32[]{:S(2)}) copy-start(f32[2,512]{1,0:T(2,128)} %get-tuple-element.7) | copy-start | bytes 12292
  116.9 5.7 %copy-start.8 = (f32[2,512]{1,0:T(2,128)S(1)}, f32[2,512]{1,0:T(2,128)}, u32[]{:S(2)}) copy-start(f32[2,512]{1,0:T(2,128)} %get-tuple-element.6) | copy-start | bytes 12292
  122.6 7.8 %copy-start.3 = (bf16[16,128,1,6,128]{4,1,0,3,2:T(8,128)(2,1)S(1)}, bf16[16,128,1,6,128]{4,1,0,3,2:T(8,128)(2,1)}, u32[]{:S(2)}) copy-start(bf16[16,128,1,6,128]{4,1,0,3,2:T(8,128)(2,1)} %copy-done.2) | copy-start | bytes 9437188
  138.2 10.7 %copy-start.6 = (f32[4096]{0:T(1024)S(1)}, f32[4096]{0:T(1024)}, u32[]{:S(2)}) copy-start(f32[4096]{0:T(1024)} %param.13) | copy-start | bytes 49156
  142.7 33.4 %all-to-all-start.1 = ((bf16[2048,1,2,128]{3,2,1,0:T(2,128)(2,1)}), bf16[2048,1,2,128]{3,2,1,0:T(2,128)(2,1)S(1)}, u32[]{:S(2)}, u32[]{:S(2)}) async-start(bf16[2048,1,2,128]{3,2,1,0:T(2,128)(2,1)} %copy.32), calls=%async_computation.1 | async-start | bytes 2097152 | tf_op jit(solution)/shard_map/all_to_all | solution.py:126
where the time goes:
time: 184 us
  waiting for transfers between devices  60.4 us (33%)
  matrix products  33.3 us (18%)
  blocking collectives  27.5 us (15%)
  local copies, waits for them, and re-layouts  21.2 us (12%)
  other arithmetic  21.2 us (12%)
  starting transfers between devices  17.3 us (9%)
  between operations  2.83 us (2%)
    all_to_all x1, waiting for transfers between devices, sent_together(): lax.all_to_all(both, axis, split_axis=split_dim, concat_axis=concat_dim,...  33.2 us
    all_to_all x1, waiting for transfers between devices, local(): lax.all_to_all(mixed, 'seq', split_axis=0, concat_axis=1, tiled=True)  27.2 us
    all_gather x1, blocking collectives, all_blocks(): tiles = lax.all_gather(tiles, axes[k])  20.1 us
    dot_general x4, matrix products, masked_scores(): jnp.einsum('qhd,khd->hqk', q_block, key_rot, preferred_element_type=jnp.f...  17.4 us
    dot_general x4, matrix products, attend(): jnp.einsum('hqk,khd->qhd', weights.astype(jnp.bfloat16), value, preferred...  15.8 us
    all_to_all x1, starting transfers between devices, sent_together(): lax.all_to_all(both, axis, split_axis=split_dim, concat_axis=concat_dim,...  11.8 us
    unnamed x27, local copies, waits for them, and re-layouts  10.6 us
    reduce_sum x1, other arithmetic, attend(): total = jnp.sum(weights, axis=-1)  7.78 us
  transfers between devices with their start and end apart: 2, of which 2 were waited for; matrix products, arithmetic and copies ran while one was open for 5% of the time, Pallas kernels for 0%

commit v1 on v0

v1 whole, which is shorter than its diff:
```python
import math

import jax
import jax.numpy as jnp
import numpy as np
from jax import lax
from jax.experimental import pallas as pl
from jax.experimental.pallas import tpu as pltpu
from jax.sharding import PartitionSpec as P

HD = 128
FRAME_TOK = 448
GRID_W = 28
LIVE = 1792
TOK = 128
EXTRA0 = 3584
MESH = pl.DeviceIdType.MESH
EXP_SCALE = HD ** (-0.5) * math.log2(math.e)
BF = jnp.bfloat16
F32 = jnp.float32
WIDE = 256


def rope_tables():
    position = np.arange(LIVE)
    frame = (position // FRAME_TOK).astype(np.float32)
    within = position % FRAME_TOK
    row_pos = (within // GRID_W).astype(np.float32)
    col_pos = (within % GRID_W).astype(np.float32)
    inv_time = 10000.0 ** (-2.0 * np.arange(22) / 44.0)
    inv_space = 10000.0 ** (-2.0 * np.arange(21) / 42.0)
    angles = np.concatenate(
        [
            frame[:, None] * inv_time[None, :],
            row_pos[:, None] * inv_space[None, :],
            col_pos[:, None] * inv_space[None, :],
        ],
        axis=1,
    )
    cosine, sine = np.cos(angles), np.sin(angles)
    table = np.stack(
        [np.concatenate([cosine, cosine], axis=1), np.concatenate([-sine, sine], axis=1)]
    )
    return table.astype(np.float32)


def kernel(
    nx,
    ny,
    compute,
    q,
    k,
    v,
    counts,
    assignment,
    timesteps,
    gain,
    table,
    out,
    qb,
    kb,
    vb,
    ob,
    qx,
    kx,
    vx,
    ox,
    kr,
    vt,
    sbuf,
    rel,
    relx,
    relo,
    relox,
    ybuf,
    xbuf,
    tab,
    lenb,
    zbuf,
    ss,
    sx,
    rs,
    rx,
    so,
    sox,
    ro,
    rox,
    rr,
    rrx,
    fs,
    fsx,
    rro,
    rrox,
    fso,
    fsox,
    ysend,
    yrecv,
    xsend,
    xrecv,
    loc,
):
    cl = lax.axis_index("clip")
    i = lax.axis_index("seq")
    z = i // 2
    c = i % 2
    y = cl % ny
    x = cl // ny
    has_x = (c == 0) & (z % 3 != 0) & (i < 14)
    slot = z - z // 4
    my_e = z - 1 - z // 3

    def chip_at(t):
        mag = (4 - t // 2) * ((t + 7) // 8)
        return (z + mag * (1 - 2 * (t % 2)) + 8) % 8

    def rcopy(src, dst, send, recv, j):
        return pltpu.make_async_remote_copy(
            src, dst, send, recv, device_id={"seq": j}, device_id_type=MESH
        )

    def arrived(view, sem):
        pltpu.make_async_copy(view, view, sem).wait()

    def rows_of(j, n=TOK):
        return pl.ds(pl.multiple_of(j * n, n), n)

    def cols(start, n):
        return pl.ds(pl.multiple_of(start, 128), n)

    barrier = pltpu.get_barrier_semaphore()

    def greet(axis, j):
        pl.semaphore_signal(barrier, inc=1, device_id={axis: j}, device_id_type=MESH)

    for dy in range(1, ny):
        greet("clip", x * ny + (y + dy) % ny)
    for dx in range(1, nx):
        greet("clip", ((x + dx) % nx) * ny + y)
    near = ny - 1 + nx - 1

    @pl.when(i < 14)
    def _():
        def one(t, carry):
            w = chip_at(t)
            for cc in (0, 1):

                @pl.when((w != 7) & (t != 1) & (2 * w + cc != i))
                def _():
                    greet("seq", 2 * w + cc)

                @pl.when((w != 7) & (t == 1))
                def _():
                    greet("seq", 14 + cc)

            return carry

        lax.fori_loop(0, 8, one, 0)
        pl.semaphore_wait(barrier, near + 13)

    @pl.when(i >= 14)
    def _():
        def one(n, carry):
            greet("seq", n + 2 * (n // 6))
            return carry

        lax.fori_loop(0, 12, one, 0)
        pl.semaphore_wait(barrier, near + 12)

    lane = lax.broadcasted_iota(jnp.int32, (8, 128), 1)
    mine = jnp.zeros((8, 128), jnp.int32)
    for m in range(4):
        mine = jnp.where(lane == 4 * cl + m, counts[m], mine)
    ybuf[y] = mine

    def ycopy(dy):
        return pltpu.make_async_remote_copy(
            ybuf.at[y],
            ybuf.at[y],
            ysend.at[dy],
            yrecv.at[y],
            device_id={"clip": x * ny + (y + dy) % ny},
            device_id_type=MESH,
        )

    def xcopy(dx):
        return pltpu.make_async_remote_copy(
            xbuf.at[x],
            xbuf.at[x],
            xsend.at[dx],
            xrecv.at[x],
            device_id={"clip": ((x + dx) % nx) * ny + y},
            device_id_type=MESH,
        )

    for dy in range(1, ny):
        ycopy(dy).start()

    arrays = ((k, kb, kx), (v, vb, vx), (q, qb, qx))

    def each_send(a, act):
        src, buf, bx = arrays[a]

        def one(tt, carry):
            t = (tt + 1) % 8
            w = chip_at(t)
            e = w - 1 - w // 3

            @pl.when((w != 7) & (t == 1))
            def _():
                act(
                    rcopy(
                        src.at[0, :, cols(512 * w, 512)],
                        rel.at[a, slot],
                        ss.at[a, 2 * w],
                        rr.at[a, slot],
                        14 + c,
                    )
                )

                @pl.when(w % 3 != 0)
                def _():
                    act(
                        rcopy(
                            src.at[0, :, cols(EXTRA0 + 128 * e, 128)],
                            relx.at[a, slot],
                            sx.at[a, e],
                            rrx.at[a, slot],
                            14 + c,
                        )
                    )

            @pl.when((w != 7) & (t != 1))
            def _():
                for cc in (0, 1):
                    j = 2 * w + cc

                    @pl.when(j != i)
                    def _():
                        act(
                            rcopy(
                                src.at[0, :, cols(256 * j, 256)],
                                buf.at[rows_of(i)],
                                ss.at[a, j],
                                rs.at[a, i],
                                j,
                            )
                        )

                @pl.when((w % 3 != 0) & (2 * w != i))
                def _():
                    act(
                        rcopy(
                            src.at[0, :, cols(EXTRA0 + 128 * e, 128)],
                            bx.at[rows_of(i)],
                            sx.at[a, e],
                            rx.at[a, i],
                            2 * w,
                        )
                    )

            return carry

        lax.fori_loop(0, 8, one, 0)

    def own_copy(a):
        src, buf, bx = arrays[a]
        pltpu.make_async_copy(
            src.at[0, :, cols(256 * i, 256)], buf.at[rows_of(i)], rs.at[a, i]
        ).start()

        @pl.when(has_x)
        def _():
            pltpu.make_async_copy(
                src.at[0, :, cols(EXTRA0 + 128 * my_e, 128)], bx.at[rows_of(i)], rx.at[a, i]
            ).start()

    def await_block(a, w):
        _, buf, bx = arrays[a]
        for cc in (0, 1):
            j = 2 * w + cc
            arrived(buf.at[rows_of(j)], rs.at[a, j])

            @pl.when(has_x)
            def _():
                arrived(bx.at[rows_of(j)], rx.at[a, j])

    def turn(block, w):
        part = pl.ds(pl.multiple_of(w * WIDE, WIDE), WIDE)
        return block * tab[0, part] + pltpu.roll(block, HD // 2, 1) * tab[1, part]

    def positions(shape, dim):
        return lax.broadcasted_iota(jnp.int32, shape, dim).astype(F32)

    def start(copy):
        copy.start()

    def each_result(w, t, act):
        part = pl.ds(pl.multiple_of(w * WIDE, WIDE), WIDE)

        @pl.when(t == 1)
        def _():
            act(rcopy(ob.at[part], relo.at[slot], so.at[2 * w], rro.at[slot], 14 + c))

            @pl.when(has_x)
            def _():
                act(rcopy(ox.at[part], relox.at[slot], sox.at[2 * w], rrox.at[slot], 14 + c))

        @pl.when(t != 1)
        def _():
            for cc in (0, 1):
                j = 2 * w + cc

                @pl.when(j != i)
                def _():
                    act(
                        rcopy(
                            ob.at[rows_of(j)],
                            out.at[0, :, cols(256 * i, 256)],
                            so.at[j],
                            ro.at[i],
                            j,
                        )
                    )

                    @pl.when(has_x)
                    def _():
                        act(
                            rcopy(
                                ox.at[rows_of(j)],
                                out.at[0, :, cols(EXTRA0 + 128 * my_e, 128)],
                                sox.at[j],
                                rox.at[my_e],
                                j,
                            )
                        )

    def gate_of(head):
        fraction = jnp.full((1, HD), timesteps[0], jnp.int32).astype(F32) / 1000.0
        sigma = 5.0 * fraction / (1.0 + 4.0 * fraction)
        return 1.0 + sigma * gain[pl.ds(head, 1), :]

    def attend(h, block, w, head):
        q_rot = turn(block.astype(F32), w).astype(BF)
        top = None
        for n in range(LIVE // WIDE):
            part = pl.ds(n * WIDE, WIDE)
            s = lax.dot_general(
                kr[h, part], q_rot, (((1,), (1,)), ((), ())), preferred_element_type=F32
            )
            sbuf[h, part] = s
            high = jnp.max(s.reshape(WIDE // 8, 8, WIDE), axis=0)
            top = high if top is None else jnp.maximum(top, high)
        top = jnp.max(top, axis=0, keepdims=True)
        total = None
        for n in range(LIVE // WIDE):
            part = pl.ds(n * WIDE, WIDE)
            p = jnp.exp2((sbuf[h, part] - top) * EXP_SCALE).astype(BF)
            term = jnp.dot(vt[h, :, part], p, preferred_element_type=F32)
            total = term if total is None else total + term
        mixed = total[:HD] * (1.0 / total[HD : HD + 1])
        mixed = jnp.transpose(mixed).astype(BF).astype(F32)
        pos = positions((WIDE, HD), 0) + (w * WIDE).astype(F32)
        return jnp.where(pos < lenb[0:1, 0:HD], mixed * gate_of(head), 0.0).astype(BF)

    @pl.when(i < 14)
    def _():
        table_copy = pltpu.make_async_copy(table, tab, loc.at[0])
        table_copy.start()
        for a in range(3):
            each_send(a, start)
            own_copy(a)
        table_copy.wait()

        def k_step(tt, carry):
            w = chip_at((8 - tt) % 8)

            @pl.when(w != 7)
            def _():
                part = pl.ds(pl.multiple_of(w * WIDE, WIDE), WIDE)
                await_block(0, w)
                for h in (0, 1):
                    kr[h, part] = turn(kb[part, h * HD : (h + 1) * HD].astype(F32), w).astype(BF)

                @pl.when(has_x)
                def _():
                    kr[2, part] = turn(kx[part].astype(F32), w).astype(BF)

            return carry

        lax.fori_loop(0, 8, k_step, 0)

    for dy in range(1, ny):
        o = (y + dy) % ny
        arrived(ybuf.at[o], yrecv.at[o])
    xbuf[x] = jnp.sum(ybuf[...], axis=0)
    for dx in range(1, nx):
        xcopy(dx).start()
    for dx in range(1, nx):
        o = (x + dx) % nx
        arrived(xbuf.at[o], xrecv.at[o])
    pool = jnp.sum(xbuf[...], axis=0)
    picked = jnp.where(lane == assignment[0], pool, 0).astype(F32)
    length = jnp.sum(picked, axis=1, keepdims=True) * float(FRAME_TOK)
    lenb[...] = jnp.broadcast_to(length, (8, WIDE))
    for dy in range(1, ny):
        ycopy(dy).wait_send()
    for dx in range(1, nx):
        xcopy(dx).wait_send()

    @pl.when(i < 14)
    def _():
        for n in range(1, 4):
            part = pl.ds(n * FRAME_TOK, FRAME_TOK)
            live = positions((FRAME_TOK, HD), 0) + float(n * FRAME_TOK) < lenb[0:1, 0:HD]
            for h in range(3):

                def patch(h=h):
                    first = kr[h, 0:16].astype(F32)[0:1]
                    kr[h, part] = jnp.where(live, kr[h, part].astype(F32), first).astype(BF)

                if h < 2:
                    patch()
                else:
                    pl.when(has_x)(patch)

        def v_step(tt, carry):
            w = chip_at((8 - tt) % 8)

            @pl.when(w != 7)
            def _():
                part = pl.ds(pl.multiple_of(w * WIDE, WIDE), WIDE)
                await_block(1, w)
                pos = positions((1, WIDE), 1) + (w * WIDE).astype(F32)
                live = pos < lenb[0:1]
                ones = jnp.broadcast_to(jnp.where(live, 1.0, 0.0), (16, WIDE)).astype(BF)

                def put(h, block):
                    turned = jnp.transpose(block.astype(F32))
                    vt[h, 0:HD, part] = jnp.where(live, turned, 0.0).astype(BF)
                    vt[h, HD : HD + 16, part] = ones

                for h in (0, 1):
                    put(h, vb[part, h * HD : (h + 1) * HD])

                @pl.when(has_x)
                def _():
                    put(2, vx[part])

            return carry

        lax.fori_loop(0, 8, v_step, 0)

        def q_step(t, carry):
            w = chip_at(t)

            @pl.when(w != 7)
            def _():
                part = pl.ds(pl.multiple_of(w * WIDE, WIDE), WIDE)
                await_block(2, w)
                if compute:
                    for h in (0, 1):
                        lanes = slice(h * HD, (h + 1) * HD)
                        ob[part, lanes] = attend(h, qb[part, lanes], w, 2 * i + h)

                    @pl.when(has_x)
                    def _():
                        ox[part] = attend(2, qx[part], w, 28 + my_e)

                each_result(w, t, start)

            return carry

        lax.fori_loop(0, 8, q_step, 0)

        own = [pltpu.make_async_copy(ob.at[rows_of(i)], out.at[0, :, cols(256 * i, 256)], loc.at[1])]
        own[0].start()
        own_x = pltpu.make_async_copy(
            ox.at[rows_of(i)], out.at[0, :, cols(EXTRA0 + 128 * my_e, 128)], loc.at[2]
        )

        @pl.when(has_x)
        def _():
            own_x.start()

        for a in range(3):
            each_send(a, lambda copy: copy.wait_send())

        def drain(t, carry):
            w = chip_at(t)

            @pl.when(w != 7)
            def _():
                each_result(w, t, lambda copy: copy.wait_send())

            return carry

        lax.fori_loop(0, 8, drain, 0)
        own[0].wait()

        @pl.when(has_x)
        def _():
            own_x.wait()

        def gather(j, carry):
            @pl.when(j != i)
            def _():
                arrived(out.at[0, :, cols(256 * j, 256)], ro.at[j])

            return carry

        lax.fori_loop(0, 14, gather, 0)

        def gather_x(e, carry):
            @pl.when(jnp.logical_not(has_x & (e == my_e)))
            def _():
                arrived(out.at[0, :, cols(EXTRA0 + 128 * e, 128)], rox.at[e])

            return carry

        lax.fori_loop(0, 4, gather_x, 0)

    @pl.when(i >= 14)
    def _():
        zbuf[...] = jnp.zeros_like(zbuf)
        blank = [
            pltpu.make_async_copy(zbuf, out.at[0, n * 16 : (n + 1) * 16], loc.at[n])
            for n in range(8)
        ]
        for copy in blank:
            copy.start()

        def forward(a, n, act):
            _, buf, bx = arrays[a]
            o = n + (n + 1) // 4
            w = (o + 4) % 8
            j = 2 * o + c
            for cc in (0, 1):
                act(
                    rcopy(
                        rel.at[a, n, :, cc * 256 : (cc + 1) * 256],
                        buf.at[rows_of(j)],
                        fs.at[a, n, cc],
                        rs.at[a, j],
                        2 * w + cc,
                    )
                )

            @pl.when(w % 3 != 0)
            def _():
                act(rcopy(relx.at[a, n], bx.at[rows_of(j)], fsx.at[a, n], rx.at[a, j], 2 * w))

        for a in range(3):

            def pass_on(n, carry, a=a):
                o = n + (n + 1) // 4
                w = (o + 4) % 8
                arrived(rel.at[a, n], rr.at[a, n])

                @pl.when(w % 3 != 0)
                def _():
                    arrived(relx.at[a, n], rrx.at[a, n])

                forward(a, n, start)
                return carry

            lax.fori_loop(0, 6, pass_on, 0)

        def forward_result(n, act):
            o = n + (n + 1) // 4
            w = (o + 4) % 8
            j = 2 * o + c
            e = o - 1 - o // 3
            for cc in (0, 1):
                act(
                    rcopy(
                        relo.at[n, cc * TOK : (cc + 1) * TOK],
                        out.at[0, :, cols(256 * j, 256)],
                        fso.at[n, cc],
                        ro.at[j],
                        2 * w + cc,
                    )
                )

            @pl.when((o % 3 != 0) & (c == 0))
            def _():
                for cc in (0, 1):
                    act(
                        rcopy(
                            relox.at[n, cc * TOK : (cc + 1) * TOK],
                            out.at[0, :, cols(EXTRA0 + 128 * e, 128)],
                            fsox.at[n, cc],
                            rox.at[e],
                            2 * w + cc,
                        )
                    )

        def pass_result(n, carry):
            o = n + (n + 1) // 4
            arrived(relo.at[n], rro.at[n])

            @pl.when((o % 3 != 0) & (c == 0))
            def _():
                arrived(relox.at[n], rrox.at[n])

            forward_result(n, start)
            return carry

        lax.fori_loop(0, 6, pass_result, 0)

        def finish(n, carry):
            for a in range(3):
                forward(a, n, lambda copy: copy.wait_send())
            forward_result(n, lambda copy: copy.wait_send())
            return carry

        lax.fori_loop(0, 6, finish, 0)
        for copy in blank:
            copy.wait()


def build(mesh, compute=True):
    clips = mesh.shape["clip"]
    ny = min(8, clips)
    nx = clips // ny
    dma = pltpu.SemaphoreType.DMA

    def local(queries, keys, values, frame_counts, assignment, timesteps, gate_gain):
        def call(*args):
            kernel(nx, ny, compute, *args)

        anywhere = pl.BlockSpec(memory_space=pl.ANY)
        scalars = pl.BlockSpec(memory_space=pltpu.SMEM)
        return pl.pallas_call(
            call,
            out_shape=jax.ShapeDtypeStruct(queries.shape, BF),
            in_specs=[anywhere] * 3
            + [scalars] * 3
            + [pl.BlockSpec(memory_space=pltpu.VMEM), anywhere],
            out_specs=anywhere,
            scratch_shapes=[pltpu.VMEM((LIVE, 256), BF)] * 4
            + [pltpu.VMEM((LIVE, HD), BF)] * 4
            + [
                pltpu.VMEM((3, LIVE, HD), BF),
                pltpu.VMEM((3, HD + 16, LIVE), BF),
                pltpu.VMEM((3, LIVE, WIDE), F32),
                pltpu.VMEM((3, 6, TOK, 512), BF),
                pltpu.VMEM((3, 6, TOK, HD), BF),
                pltpu.VMEM((6, WIDE, 256), BF),
                pltpu.VMEM((6, WIDE, HD), BF),
                pltpu.VMEM((ny, 8, 128), jnp.int32),
                pltpu.VMEM((nx, 8, 128), jnp.int32),
                pltpu.VMEM((2, LIVE, HD), F32),
                pltpu.VMEM((8, WIDE), F32),
                pltpu.VMEM((16, 4096), BF),
                dma((3, 14)),
                dma((3, 4)),
                dma((3, 14)),
                dma((3, 14)),
                dma((14,)),
                dma((14,)),
                dma((14,)),
                dma((4,)),
                dma((3, 6)),
                dma((3, 6)),
                dma((3, 6, 2)),
                dma((3, 6)),
                dma((6,)),
                dma((6,)),
                dma((6, 2)),
                dma((6, 2)),
                dma((8,)),
                dma((8,)),
                dma((4,)),
                dma((4,)),
                dma((8,)),
            ],
            compiler_params=pltpu.CompilerParams(
                collective_id=0, has_side_effects=True, vmem_limit_bytes=63 * 2**20
            ),
            cost_estimate=pl.CostEstimate(
                flops=4 * 1792 * 1792 * 256,
                bytes_accessed=8 * 2**20,
                transcendentals=2 * 1792 * 1792,
            ),
        )(
            queries,
            keys,
            values,
            frame_counts,
            assignment,
            timesteps,
            gate_gain.reshape(32, HD),
            jnp.asarray(rope_tables()),
        )

    tokens = P("clip", "seq", None)
    return jax.shard_map(
        local,
        mesh=mesh,
        in_specs=(tokens, tokens, tokens, P("clip"), P("clip"), P("clip"), P()),
        out_specs=tokens,
        check_vma=False,
    )


def solution(mesh):
    return build(mesh)
```

time: 184 us -> 116 us (0.63)
  the two profiles are of different devices: /device:TPU:1 before, /device:TPU:135 now
where the time goes in v1:
time: 116 us
  Pallas kernels  113 us (97%)
  local copies, waits for them, and re-layouts  2.29 us (2%)
  between operations  1.3 us (1%)
    pallas_call x1, Pallas kernels, local(): pl.pallas_call(call, out_shape=jax.ShapeDtypeStruct(queries.shape, BF), i...  113 us

profile of v1, /device:TPU:135, one launch (start us, length us, event | category | flops | bytes accessed | tf_op | source)
XLA Modules:
  0.0 116.3 jit_solution(5244942242657875236)
XLA Ops:
  1.3 112.7 %shard_map.82 = bf16[1,128,4096]{2,1,0:T(8,128)(2,1)} custom-call(bf16[1,128,4096]{2,1,0:T(8,128)(2,1)} %args_0_.4, bf16[1,128,4096]{2,1,0:T(8,128)(2,1)} %args_1_.4, bf16[1,128,4096]{2,1,0:T(8,128)(2,1)} %args_2_.4, s32[4]{0:T(128)} %args_3_.4, s32[1]{0:T(128)S(6)} %copy.10.args_4_, s32[1]{0:T(128)S(6)} %copy.11.args_5_, f32[32,128]{1,0:T(8,128)} %bitcast.1, ...), custom_call_target="tpu_custom_call" | custom-call | flops 3288334336 | bytes 8388608 | tf_op jit(solution)/shard_map/pallas_call | solution.py:633
  114.0 2.3 %copy.12 = bf16[1,128,4096]{2,1,0:T(8,128)(2,1)} copy(bf16[1,128,4096]{2,1,0:T(8,128)(2,1)} %shard_map.82) | data formatting | bytes 2097152

commit v2 on v1

--- a/solution.py
+++ b/solution.py
@@ -47,7 +47,6 @@
 def kernel(
     nx,
     ny,
-    compute,
     q,
     k,
     v,
@@ -106,7 +105,8 @@
     y = cl % ny
     x = cl // ny
     has_x = (c == 0) & (z % 3 != 0) & (i < 14)
-    slot = z - z // 4
+    slot = z // 2
+    relayed = (z == 0) | (z == 2) | (z == 5)
     my_e = z - 1 - z // 3
 
     def chip_at(t):
@@ -138,33 +138,15 @@
         greet("clip", ((x + dx) % nx) * ny + y)
     near = ny - 1 + nx - 1
 
-    @pl.when(i < 14)
-    def _():
-        def one(t, carry):
-            w = chip_at(t)
-            for cc in (0, 1):
-
-                @pl.when((w != 7) & (t != 1) & (2 * w + cc != i))
-                def _():
-                    greet("seq", 2 * w + cc)
-
-                @pl.when((w != 7) & (t == 1))
-                def _():
-                    greet("seq", 14 + cc)
-
-            return carry
-
-        lax.fori_loop(0, 8, one, 0)
-        pl.semaphore_wait(barrier, near + 13)
-
-    @pl.when(i >= 14)
-    def _():
-        def one(n, carry):
-            greet("seq", n + 2 * (n // 6))
-            return carry
-
-        lax.fori_loop(0, 12, one, 0)
-        pl.semaphore_wait(barrier, near + 12)
+    def one(n, carry):
+        @pl.when((n != i) & ((n < 14) | (i < 14)))
+        def _():
+            greet("seq", n)
+
+        return carry
+
+    lax.fori_loop(0, 16, one, 0)
+    pl.semaphore_wait(barrier, near + 15 - i // 14)
 
     lane = lax.broadcasted_iota(jnp.int32, (8, 128), 1)
     mine = jnp.zeros((8, 128), jnp.int32)
@@ -204,59 +186,33 @@
             t = (tt + 1) % 8
             w = chip_at(t)
             e = w - 1 - w // 3
-
-            @pl.when((w != 7) & (t == 1))
-            def _():
-                act(
-                    rcopy(
-                        src.at[0, :, cols(512 * w, 512)],
-                        rel.at[a, slot],
-                        ss.at[a, 2 * w],
-                        rr.at[a, slot],
-                        14 + c,
-                    )
-                )
+            via = (t == 1) & relayed
+
+            @pl.when(w != 7)
+            def _():
+                for cc in (0, 1):
+                    j = 2 * w + cc
+                    piece = src.at[0, :, cols(256 * j, 256)]
+
+                    @pl.when(via)
+                    def _():
+                        act(rcopy(piece, rel.at[a, slot, cc], ss.at[a, j], rr.at[a, slot, cc], 14 + c))
+
+                    @pl.when((j != i) & jnp.logical_not(via))
+                    def _():
+                        act(rcopy(piece, buf.at[rows_of(i)], ss.at[a, j], rs.at[a, i], j))
 
                 @pl.when(w % 3 != 0)
                 def _():
-                    act(
-                        rcopy(
-                            src.at[0, :, cols(EXTRA0 + 128 * e, 128)],
-                            relx.at[a, slot],
-                            sx.at[a, e],
-                            rrx.at[a, slot],
-                            14 + c,
-                        )
-                    )
-
-            @pl.when((w != 7) & (t != 1))
-            def _():
-                for cc in (0, 1):
-                    j = 2 * w + cc
-
-                    @pl.when(j != i)
+                    piece = src.at[0, :, cols(EXTRA0 + 128 * e, 128)]
+
+                    @pl.when(via)
                     def _():
-                        act(
-                            rcopy(
-                                src.at[0, :, cols(256 * j, 256)],
-                                buf.at[rows_of(i)],
-                                ss.at[a, j],
-                                rs.at[a, i],
-                                j,
-                            )
-                        )
-
-                @pl.when((w % 3 != 0) & (2 * w != i))
-                def _():
-                    act(
-                        rcopy(
-                            src.at[0, :, cols(EXTRA0 + 128 * e, 128)],
-                            bx.at[rows_of(i)],
-                            sx.at[a, e],
-                            rx.at[a, i],
-                            2 * w,
-                        )
-                    )
+                        act(rcopy(piece, relx.at[a, slot], sx.at[a, e], rrx.at[a, slot], 14 + c))
+
+                    @pl.when((2 * w != i) & jnp.logical_not(via))
+                    def _():
+                        act(rcopy(piece, bx.at[rows_of(i)], sx.at[a, e], rx.at[a, i], 2 * w))
 
             return carry
 
@@ -295,44 +251,34 @@
         copy.start()
 
     def each_result(w, t, act):
-        part = pl.ds(pl.multiple_of(w * WIDE, WIDE), WIDE)
-
-        @pl.when(t == 1)
-        def _():
-            act(rcopy(ob.at[part], relo.at[slot], so.at[2 * w], rro.at[slot], 14 + c))
-
-            @pl.when(has_x)
-            def _():
-                act(rcopy(ox.at[part], relox.at[slot], sox.at[2 * w], rrox.at[slot], 14 + c))
-
-        @pl.when(t != 1)
-        def _():
-            for cc in (0, 1):
-                j = 2 * w + cc
-
-                @pl.when(j != i)
+        via = (t == 1) & relayed
+        for cc in (0, 1):
+            j = 2 * w + cc
+            rows = rows_of(j)
+
+            @pl.when(via)
+            def _():
+                act(rcopy(ob.at[rows], relo.at[slot, cc], so.at[j], rro.at[slot, cc], 14 + c))
+
+                @pl.when(has_x)
+                def _():
+                    act(rcopy(ox.at[rows], relox.at[slot, cc], sox.at[j], rrox.at[slot, cc], 14 + c))
+
+            @pl.when((j != i) & jnp.logical_not(via))
+            def _():
+                act(rcopy(ob.at[rows], out.at[0, :, cols(256 * i, 256)], so.at[j], ro.at[i], j))
+
+                @pl.when(has_x)
                 def _():
                     act(
                         rcopy(
-                            ob.at[rows_of(j)],
-                            out.at[0, :, cols(256 * i, 256)],
-                            so.at[j],
-                            ro.at[i],
+                            ox.at[rows],
+                            out.at[0, :, cols(EXTRA0 + 128 * my_e, 128)],
+                            sox.at[j],
+                            rox.at[my_e],
                             j,
                         )
                     )
-
-                    @pl.when(has_x)
-                    def _():
-                        act(
-                            rcopy(
-                                ox.at[rows_of(j)],
-                                out.at[0, :, cols(EXTRA0 + 128 * my_e, 128)],
-                                sox.at[j],
-                                rox.at[my_e],
-                                j,
-                            )
-                        )
 
     def gate_of(head):
         fraction = jnp.full((1, HD), timesteps[0], jnp.int32).astype(F32) / 1000.0
@@ -389,6 +335,36 @@
 
         lax.fori_loop(0, 8, k_step, 0)
 
+    def source_of(n):
+        return 2 * n + n // 2
+
+    def forward(a, n, act, wait):
+        _, buf, bx = arrays[a]
+        o = source_of(n)
+        w = (o + 4) % 8
+        rows = rows_of(2 * o + c)
+        for cc in (0, 1):
+            if wait:
+                arrived(rel.at[a, n, cc], rr.at[a, n, cc])
+            act(rcopy(rel.at[a, n, cc], buf.at[rows], fs.at[a, n, cc], rs.at[a, 2 * o + c], 2 * w + cc))
+
+        @pl.when(w % 3 != 0)
+        def _():
+            if wait:
+                arrived(relx.at[a, n], rrx.at[a, n])
+            act(rcopy(relx.at[a, n], bx.at[rows], fsx.at[a, n], rx.at[a, 2 * o + c], 2 * w))
+
+    def relay(a):
+        def pass_on(n, carry):
+            forward(a, n, start, True)
+            return carry
+
+        lax.fori_loop(0, 3, pass_on, 0)
+
+    @pl.when(i >= 14)
+    def _():
+        relay(0)
+
     for dy in range(1, ny):
         o = (y + dy) % ny
         arrived(ybuf.at[o], yrecv.at[o])
@@ -450,21 +426,21 @@
 
         lax.fori_loop(0, 8, v_step, 0)
 
-        def q_step(t, carry):
+        def q_step(tt, carry):
+            t = ((tt % 7) + 1) * ((tt + 6) // 7)
             w = chip_at(t)
 
             @pl.when(w != 7)
             def _():
                 part = pl.ds(pl.multiple_of(w * WIDE, WIDE), WIDE)
                 await_block(2, w)
-                if compute:
-                    for h in (0, 1):
-                        lanes = slice(h * HD, (h + 1) * HD)
-                        ob[part, lanes] = attend(h, qb[part, lanes], w, 2 * i + h)
-
-                    @pl.when(has_x)
-                    def _():
-                        ox[part] = attend(2, qx[part], w, 28 + my_e)
+                for h in (0, 1):
+                    lanes = slice(h * HD, (h + 1) * HD)
+                    ob[part, lanes] = attend(h, qb[part, lanes], w, 2 * i + h)
+
+                @pl.when(has_x)
+                def _():
+                    ox[part] = attend(2, qx[part], w, 28 + my_e)
 
                 each_result(w, t, start)
 
@@ -521,6 +497,8 @@
 
     @pl.when(i >= 14)
     def _():
+        relay(1)
+        relay(2)
         zbuf[...] = jnp.zeros_like(zbuf)
         blank = [
             pltpu.make_async_copy(zbuf, out.at[0, n * 16 : (n + 1) * 16], loc.at[n])
@@ -529,96 +507,53 @@
         for copy in blank:
             copy.start()
 
-        def forward(a, n, act):
-            _, buf, bx = arrays[a]
-            o = n + (n + 1) // 4
+        def forward_result(n, cc, act, wait):
+            o = source_of(n)
             w = (o + 4) % 8
             j = 2 * o + c
-            for cc in (0, 1):
+            e = o - 1 - o // 3
+            if wait:
+                arrived(relo.at[n, cc], rro.at[n, cc])
+            act(
+                rcopy(
+                    relo.at[n, cc], out.at[0, :, cols(256 * j, 256)], fso.at[n, cc], ro.at[j], 2 * w + cc
+                )
+            )
+
+            @pl.when((o % 3 != 0) & (c == 0))
+            def _():
+                if wait:
+                    arrived(relox.at[n, cc], rrox.at[n, cc])
                 act(
                     rcopy(
-                        rel.at[a, n, :, cc * 256 : (cc + 1) * 256],
-                        buf.at[rows_of(j)],
-                        fs.at[a, n, cc],
-                        rs.at[a, j],
+                        relox.at[n, cc],
+                        out.at[0, :, cols(EXTRA0 + 128 * e, 128)],
+                        fsox.at[n, cc],
+                        rox.at[e],
                         2 * w + cc,
                     )
                 )
 
-            @pl.when(w % 3 != 0)
-            def _():
-                act(rcopy(relx.at[a, n], bx.at[rows_of(j)], fsx.at[a, n], rx.at[a, j], 2 * w))
-
-        for a in range(3):
-
-            def pass_on(n, carry, a=a):
-                o = n + (n + 1) // 4
-                w = (o + 4) % 8
-                arrived(rel.at[a, n], rr.at[a, n])
-
-                @pl.when(w % 3 != 0)
-                def _():
-                    arrived(relx.at[a, n], rrx.at[a, n])
-
-                forward(a, n, start)
-                return carry
-
-            lax.fori_loop(0, 6, pass_on, 0)
-
-        def forward_result(n, act):
-            o = n + (n + 1) // 4
-            w = (o + 4) % 8
-            j = 2 * o + c
-            e = o - 1 - o // 3
+        def pass_result(n, carry):
             for cc in (0, 1):
-                act(
-                    rcopy(
-                        relo.at[n, cc * TOK : (cc + 1) * TOK],
-                        out.at[0, :, cols(256 * j, 256)],
-                        fso.at[n, cc],
-                        ro.at[j],
-                        2 * w + cc,
-                    )
-                )
-
-            @pl.when((o % 3 != 0) & (c == 0))
-            def _():
-                for cc in (0, 1):
-                    act(
-                        rcopy(
-                            relox.at[n, cc * TOK : (cc + 1) * TOK],
-                            out.at[0, :, cols(EXTRA0 + 128 * e, 128)],
-                            fsox.at[n, cc],
-                            rox.at[e],
-                            2 * w + cc,
-                        )
-                    )
-
-        def pass_result(n, carry):
-            o = n + (n + 1) // 4
-            arrived(relo.at[n], rro.at[n])
-
-            @pl.when((o % 3 != 0) & (c == 0))
-            def _():
-                arrived(relox.at[n], rrox.at[n])
-
-            forward_result(n, start)
-            return carry
-
-        lax.fori_loop(0, 6, pass_result, 0)
+                forward_result(n, cc, start, True)
+            return carry
+
+        lax.fori_loop(0, 3, pass_result, 0)
 
         def finish(n, carry):
             for a in range(3):
-                forward(a, n, lambda copy: copy.wait_send())
-            forward_result(n, lambda copy: copy.wait_send())
-            return carry
-
-        lax.fori_loop(0, 6, finish, 0)
+                forward(a, n, lambda copy: copy.wait_send(), False)
+            for cc in (0, 1):
+                forward_result(n, cc, lambda copy: copy.wait_send(), False)
+            return carry
+
+        lax.fori_loop(0, 3, finish, 0)
         for copy in blank:
             copy.wait()
 
 
-def build(mesh, compute=True):
+def build(mesh):
     clips = mesh.shape["clip"]
     ny = min(8, clips)
     nx = clips // ny
@@ -626,7 +561,7 @@
 
     def local(queries, keys, values, frame_counts, assignment, timesteps, gate_gain):
         def call(*args):
-            kernel(nx, ny, compute, *args)
+            kernel(nx, ny, *args)
 
         anywhere = pl.BlockSpec(memory_space=pl.ANY)
         scalars = pl.BlockSpec(memory_space=pltpu.SMEM)
@@ -643,10 +578,10 @@
                 pltpu.VMEM((3, LIVE, HD), BF),
                 pltpu.VMEM((3, HD + 16, LIVE), BF),
                 pltpu.VMEM((3, LIVE, WIDE), F32),
-                pltpu.VMEM((3, 6, TOK, 512), BF),
-                pltpu.VMEM((3, 6, TOK, HD), BF),
-                pltpu.VMEM((6, WIDE, 256), BF),
-                pltpu.VMEM((6, WIDE, HD), BF),
+                pltpu.VMEM((3, 3, 2, TOK, 256), BF),
+                pltpu.VMEM((3, 3, TOK, HD), BF),
+                pltpu.VMEM((3, 2, TOK, 256), BF),
+                pltpu.VMEM((3, 2, TOK, HD), BF),
                 pltpu.VMEM((ny, 8, 128), jnp.int32),
                 pltpu.VMEM((nx, 8, 128), jnp.int32),
                 pltpu.VMEM((2, LIVE, HD), F32),
@@ -660,14 +595,14 @@
                 dma((14,)),
                 dma((14,)),
                 dma((4,)),
-                dma((3, 6)),
-                dma((3, 6)),
-                dma((3, 6, 2)),
-                dma((3, 6)),
-                dma((6,)),
-                dma((6,)),
-                dma((6, 2)),
-                dma((6, 2)),
+                dma((3, 3, 2)),
+                dma((3, 3)),
+                dma((3, 3, 2)),
+                dma((3, 3)),
+                dma((3, 2)),
+                dma((3, 2)),
+                dma((3, 2)),
+                dma((3, 2)),
                 dma((8,)),
                 dma((8,)),
                 dma((4,)),

time: 116 us -> 110 us (0.948)
  the two profiles are of different devices: /device:TPU:135 before, /device:TPU:71 now
where the time goes in v2:
time: 110 us
  Pallas kernels  106 us (96%)
  local copies, waits for them, and re-layouts  2.29 us (2%)
  between operations  1.3 us (1%)
    pallas_call x1, Pallas kernels, local(): pl.pallas_call(call, out_shape=jax.ShapeDtypeStruct(queries.shape, BF), i...  106 us
    unnamed x1, local copies, waits for them, and re-layouts  2.29 us

profile of v2, /device:TPU:71, one launch (start us, length us, event | category | flops | bytes accessed | tf_op | source)
XLA Modules:
  0.0 110.0 jit_solution(5735251014723872287)
XLA Ops:
  1.3 106.4 %shard_map.82 = bf16[1,128,4096]{2,1,0:T(8,128)(2,1)} custom-call(bf16[1,128,4096]{2,1,0:T(8,128)(2,1)} %args_0_.4, bf16[1,128,4096]{2,1,0:T(8,128)(2,1)} %args_1_.4, bf16[1,128,4096]{2,1,0:T(8,128)(2,1)} %args_2_.4, s32[4]{0:T(128)} %args_3_.4, s32[1]{0:T(128)S(6)} %copy.10.args_4_, s32[1]{0:T(128)S(6)} %copy.11.args_5_, f32[32,128]{1,0:T(8,128)} %bitcast.1, ...), custom_call_target="tpu_custom_call" | custom-call | flops 3288334336 | bytes 8388608 | tf_op jit(solution)/shard_map/pallas_call | solution.py:568
  107.7 2.3 %copy.12 = bf16[1,128,4096]{2,1,0:T(8,128)(2,1)} copy(bf16[1,128,4096]{2,1,0:T(8,128)(2,1)} %shard_map.82) | data formatting | bytes 2097152

commit v3 on v2

--- a/solution.py
+++ b/solution.py
@@ -14,6 +14,8 @@
 LIVE = 1792
 TOK = 128
 EXTRA0 = 3584
+COUNTER = 14
+RELAY = 15
 MESH = pl.DeviceIdType.MESH
 EXP_SCALE = HD ** (-0.5) * math.log2(math.e)
 BF = jnp.bfloat16
@@ -97,6 +99,9 @@
     xsend,
     xrecv,
     loc,
+    lsend,
+    lrecv,
+    ready,
 ):
     cl = lax.axis_index("clip")
     i = lax.axis_index("seq")
@@ -132,71 +137,84 @@
     def greet(axis, j):
         pl.semaphore_signal(barrier, inc=1, device_id={axis: j}, device_id_type=MESH)
 
-    for dy in range(1, ny):
-        greet("clip", x * ny + (y + dy) % ny)
-    for dx in range(1, nx):
-        greet("clip", ((x + dx) % nx) * ny + y)
+    def tell(j):
+        pl.semaphore_signal(ready.at[i], inc=1, device_id={"seq": j}, device_id_type=MESH)
+
     near = ny - 1 + nx - 1
 
-    def one(n, carry):
-        @pl.when((n != i) & ((n < 14) | (i < 14)))
+    @pl.when(i == COUNTER)
+    def _():
+        for dy in range(1, ny):
+            greet("clip", x * ny + (y + dy) % ny)
+        for dx in range(1, nx):
+            greet("clip", ((x + dx) % nx) * ny + y)
+
+    @pl.when(i < 14)
+    def _():
+        def one(n, carry):
+            @pl.when(n > i)
+            def _():
+                greet("seq", n)
+
+            return carry
+
+        lax.fori_loop(0, 16, one, 0)
+
+        @pl.when(i > 0)
         def _():
-            greet("seq", n)
-
-        return carry
-
-    lax.fori_loop(0, 16, one, 0)
-    pl.semaphore_wait(barrier, near + 15 - i // 14)
-
-    lane = lax.broadcasted_iota(jnp.int32, (8, 128), 1)
-    mine = jnp.zeros((8, 128), jnp.int32)
-    for m in range(4):
-        mine = jnp.where(lane == 4 * cl + m, counts[m], mine)
-    ybuf[y] = mine
-
-    def ycopy(dy):
-        return pltpu.make_async_remote_copy(
-            ybuf.at[y],
-            ybuf.at[y],
-            ysend.at[dy],
-            yrecv.at[y],
-            device_id={"clip": x * ny + (y + dy) % ny},
-            device_id_type=MESH,
-        )
-
-    def xcopy(dx):
-        return pltpu.make_async_remote_copy(
-            xbuf.at[x],
-            xbuf.at[x],
-            xsend.at[dx],
-            xrecv.at[x],
-            device_id={"clip": ((x + dx) % nx) * ny + y},
-            device_id_type=MESH,
-        )
-
-    for dy in range(1, ny):
-        ycopy(dy).start()
+            pl.semaphore_wait(barrier, i)
+
+        def back(n, carry):
+            @pl.when(n < i)
+            def _():
+                tell(n)
+
+            return carry
+
+        lax.fori_loop(0, 14, back, 0)
+
+    @pl.when(i == COUNTER)
+    def _():
+        pl.semaphore_wait(barrier, 14 + near)
+
+    @pl.when(i == RELAY)
+    def _():
+        pl.semaphore_wait(barrier, 14)
+        for o in (0, 2, 5):
+            for cc in (0, 1):
+                tell(2 * o + cc)
 
     arrays = ((k, kb, kx), (v, vb, vx), (q, qb, qx))
 
-    def each_send(a, act):
+    def each_send(a, act, first=False):
         src, buf, bx = arrays[a]
 
         def one(tt, carry):
-            t = (tt + 1) % 8
-            w = chip_at(t)
+            below = (8 + z - tt) // 8
+            w = below * (z - tt) + (1 - below) * tt if first else chip_at((tt + 1) % 8)
             e = w - 1 - w // 3
-            via = (t == 1) & relayed
+            via = (w == (z + 4) % 8) & relayed
 
             @pl.when(w != 7)
             def _():
                 for cc in (0, 1):
                     j = 2 * w + cc
                     piece = src.at[0, :, cols(256 * j, 256)]
+                    if first:
+
+                        @pl.when(j > i)
+                        def _():
+                            pl.semaphore_wait(ready.at[j], 1)
+
+                        if cc == 0:
+
+                            @pl.when(via)
+                            def _():
+                                pl.semaphore_wait(ready.at[RELAY], 1)
 
                     @pl.when(via)
                     def _():
-                        act(rcopy(piece, rel.at[a, slot, cc], ss.at[a, j], rr.at[a, slot, cc], 14 + c))
+                        act(rcopy(piece, rel.at[a, slot, c, cc], ss.at[a, j], rr.at[a, slot, c, cc], RELAY))
 
                     @pl.when((j != i) & jnp.logical_not(via))
                     def _():
@@ -208,7 +226,7 @@
 
                     @pl.when(via)
                     def _():
-                        act(rcopy(piece, relx.at[a, slot], sx.at[a, e], rrx.at[a, slot], 14 + c))
+                        act(rcopy(piece, relx.at[a, slot, c], sx.at[a, e], rrx.at[a, slot, c], RELAY))
 
                     @pl.when((2 * w != i) & jnp.logical_not(via))
                     def _():
@@ -258,11 +276,11 @@
 
             @pl.when(via)
             def _():
-                act(rcopy(ob.at[rows], relo.at[slot, cc], so.at[j], rro.at[slot, cc], 14 + c))
+                act(rcopy(ob.at[rows], relo.at[slot, c, cc], so.at[j], rro.at[slot, c, cc], RELAY))
 
                 @pl.when(has_x)
                 def _():
-                    act(rcopy(ox.at[rows], relox.at[slot, cc], sox.at[j], rrox.at[slot, cc], 14 + c))
+                    act(rcopy(ox.at[rows], relox.at[slot, cc], sox.at[j], rrox.at[slot, cc], RELAY))
 
             @pl.when((j != i) & jnp.logical_not(via))
             def _():
@@ -313,7 +331,7 @@
         table_copy = pltpu.make_async_copy(table, tab, loc.at[0])
         table_copy.start()
         for a in range(3):
-            each_send(a, start)
+            each_send(a, start, a == 0)
             own_copy(a)
         table_copy.wait()
 
@@ -342,17 +360,22 @@
         _, buf, bx = arrays[a]
         o = source_of(n)
         w = (o + 4) % 8
-        rows = rows_of(2 * o + c)
-        for cc in (0, 1):
-            if wait:
-                arrived(rel.at[a, n, cc], rr.at[a, n, cc])
-            act(rcopy(rel.at[a, n, cc], buf.at[rows], fs.at[a, n, cc], rs.at[a, 2 * o + c], 2 * w + cc))
-
-        @pl.when(w % 3 != 0)
-        def _():
-            if wait:
-                arrived(relx.at[a, n], rrx.at[a, n])
-            act(rcopy(relx.at[a, n], bx.at[rows], fsx.at[a, n], rx.at[a, 2 * o + c], 2 * w))
+        for oc in (0, 1):
+            j = 2 * o + oc
+            for cc in (0, 1):
+                if wait:
+                    arrived(rel.at[a, n, oc, cc], rr.at[a, n, oc, cc])
+                act(
+                    rcopy(
+                        rel.at[a, n, oc, cc], buf.at[rows_of(j)], fs.at[a, n, oc, cc], rs.at[a, j], 2 * w + cc
+                    )
+                )
+
+            @pl.when(w % 3 != 0)
+            def _():
+                if wait:
+                    arrived(relx.at[a, n, oc], rrx.at[a, n, oc])
+                act(rcopy(relx.at[a, n, oc], bx.at[rows_of(j)], fsx.at[a, n, oc], rx.at[a, j], 2 * w))
 
     def relay(a):
         def pass_on(n, carry):
@@ -361,30 +384,75 @@
 
         lax.fori_loop(0, 3, pass_on, 0)
 
-    @pl.when(i >= 14)
+    @pl.when(i == RELAY)
     def _():
         relay(0)
-
-    for dy in range(1, ny):
-        o = (y + dy) % ny
-        arrived(ybuf.at[o], yrecv.at[o])
-    xbuf[x] = jnp.sum(ybuf[...], axis=0)
-    for dx in range(1, nx):
-        xcopy(dx).start()
-    for dx in range(1, nx):
-        o = (x + dx) % nx
-        arrived(xbuf.at[o], xrecv.at[o])
-    pool = jnp.sum(xbuf[...], axis=0)
-    picked = jnp.where(lane == assignment[0], pool, 0).astype(F32)
-    length = jnp.sum(picked, axis=1, keepdims=True) * float(FRAME_TOK)
-    lenb[...] = jnp.broadcast_to(length, (8, WIDE))
-    for dy in range(1, ny):
-        ycopy(dy).wait_send()
-    for dx in range(1, nx):
-        xcopy(dx).wait_send()
+        relay(1)
+        relay(2)
+
+    @pl.when(i == COUNTER)
+    def _():
+        lane = lax.broadcasted_iota(jnp.int32, (8, 128), 1)
+        mine = jnp.zeros((8, 128), jnp.int32)
+        for m in range(4):
+            mine = jnp.where(lane == 4 * cl + m, counts[m], mine)
+        ybuf[y] = mine
+
+        def ycopy(dy):
+            return pltpu.make_async_remote_copy(
+                ybuf.at[y],
+                ybuf.at[y],
+                ysend.at[dy],
+                yrecv.at[y],
+                device_id={"clip": x * ny + (y + dy) % ny},
+                device_id_type=MESH,
+            )
+
+        def xcopy(dx):
+            return pltpu.make_async_remote_copy(
+                xbuf.at[x],
+                xbuf.at[x],
+                xsend.at[dx],
+                xrecv.at[x],
+                device_id={"clip": ((x + dx) % nx) * ny + y},
+                device_id_type=MESH,
+            )
+
+        for dy in range(1, ny):
+            ycopy(dy).start()
+        for dy in range(1, ny):
+            o = (y + dy) % ny
+            arrived(ybuf.at[o], yrecv.at[o])
+        xbuf[x] = jnp.sum(ybuf[...], axis=0)
+        for dx in range(1, nx):
+            xcopy(dx).start()
+        for dx in range(1, nx):
+            o = (x + dx) % nx
+            arrived(xbuf.at[o], xrecv.at[o])
+        pool = jnp.sum(xbuf[...], axis=0)
+        picked = jnp.where(lane == assignment[0], pool, 0).astype(F32)
+        length = jnp.sum(picked, axis=1, keepdims=True) * float(FRAME_TOK)
+        lenb[...] = jnp.broadcast_to(length, (8, WIDE))
+
+        def publish(n, carry):
+            rcopy(lenb, lenb, lsend.at[n], lrecv.at[0], n).start()
+            return carry
+
+        lax.fori_loop(0, 14, publish, 0)
+        for dy in range(1, ny):
+            ycopy(dy).wait_send()
+        for dx in range(1, nx):
+            xcopy(dx).wait_send()
+
+        def published(n, carry):
+            rcopy(lenb, lenb, lsend.at[n], lrecv.at[0], n).wait_send()
+            return carry
+
+        lax.fori_loop(0, 14, published, 0)
 
     @pl.when(i < 14)
     def _():
+        arrived(lenb, lrecv.at[0])
         for n in range(1, 4):
             part = pl.ds(n * FRAME_TOK, FRAME_TOK)
             live = positions((FRAME_TOK, HD), 0) + float(n * FRAME_TOK) < lenb[0:1, 0:HD]
@@ -427,7 +495,10 @@
         lax.fori_loop(0, 8, v_step, 0)
 
         def q_step(tt, carry):
-            t = ((tt % 7) + 1) * ((tt + 6) // 7)
+            perm = [0, 2, 3, 1, 4, 5, 6, 7]
+            t = perm[7]
+            for step in range(7):
+                t = jnp.where(tt == step, perm[step], t)
             w = chip_at(t)
 
             @pl.when(w != 7)
@@ -497,8 +568,6 @@
 
     @pl.when(i >= 14)
     def _():
-        relay(1)
-        relay(2)
         zbuf[...] = jnp.zeros_like(zbuf)
         blank = [
             pltpu.make_async_copy(zbuf, out.at[0, n * 16 : (n + 1) * 16], loc.at[n])
@@ -506,37 +575,46 @@
         ]
         for copy in blank:
             copy.start()
-
-        def forward_result(n, cc, act, wait):
+        for copy in blank:
+            copy.wait()
+
+    @pl.when(i == RELAY)
+    def _():
+        def forward_result(n, act, wait):
             o = source_of(n)
             w = (o + 4) % 8
-            j = 2 * o + c
             e = o - 1 - o // 3
-            if wait:
-                arrived(relo.at[n, cc], rro.at[n, cc])
-            act(
-                rcopy(
-                    relo.at[n, cc], out.at[0, :, cols(256 * j, 256)], fso.at[n, cc], ro.at[j], 2 * w + cc
-                )
-            )
-
-            @pl.when((o % 3 != 0) & (c == 0))
-            def _():
-                if wait:
-                    arrived(relox.at[n, cc], rrox.at[n, cc])
-                act(
-                    rcopy(
-                        relox.at[n, cc],
-                        out.at[0, :, cols(EXTRA0 + 128 * e, 128)],
-                        fsox.at[n, cc],
-                        rox.at[e],
-                        2 * w + cc,
+            for cc in (0, 1):
+                for oc in (0, 1):
+                    j = 2 * o + oc
+                    if wait:
+                        arrived(relo.at[n, oc, cc], rro.at[n, oc, cc])
+                    act(
+                        rcopy(
+                            relo.at[n, oc, cc],
+                            out.at[0, :, cols(256 * j, 256)],
+                            fso.at[n, oc, cc],
+                            ro.at[j],
+                            2 * w + cc,
+                        )
                     )
-                )
+
+                @pl.when(o % 3 != 0)
+                def _():
+                    if wait:
+                        arrived(relox.at[n, cc], rrox.at[n, cc])
+                    act(
+                        rcopy(
+                            relox.at[n, cc],
+                            out.at[0, :, cols(EXTRA0 + 128 * e, 128)],
+                            fsox.at[n, cc],
+                            rox.at[e],
+                            2 * w + cc,
+                        )
+                    )
 
         def pass_result(n, carry):
-            for cc in (0, 1):
-                forward_result(n, cc, start, True)
+            forward_result(n, start, True)
             return carry
 
         lax.fori_loop(0, 3, pass_result, 0)
@@ -544,13 +622,10 @@
         def finish(n, carry):
             for a in range(3):
                 forward(a, n, lambda copy: copy.wait_send(), False)
-            for cc in (0, 1):
-                forward_result(n, cc, lambda copy: copy.wait_send(), False)
+            forward_result(n, lambda copy: copy.wait_send(), False)
             return carry
 
         lax.fori_loop(0, 3, finish, 0)
-        for copy in blank:
-            copy.wait()
 
 
 def build(mesh):
@@ -578,9 +653,9 @@
                 pltpu.VMEM((3, LIVE, HD), BF),
                 pltpu.VMEM((3, HD + 16, LIVE), BF),
                 pltpu.VMEM((3, LIVE, WIDE), F32),
-                pltpu.VMEM((3, 3, 2, TOK, 256), BF),
-                pltpu.VMEM((3, 3, TOK, HD), BF),
-                pltpu.VMEM((3, 2, TOK, 256), BF),
+                pltpu.VMEM((3, 3, 2, 2, TOK, 256), BF),
+                pltpu.VMEM((3, 3, 2, TOK, HD), BF),
+                pltpu.VMEM((3, 2, 2, TOK, 256), BF),
                 pltpu.VMEM((3, 2, TOK, HD), BF),
                 pltpu.VMEM((ny, 8, 128), jnp.int32),
                 pltpu.VMEM((nx, 8, 128), jnp.int32),
@@ -595,19 +670,22 @@
                 dma((14,)),
                 dma((14,)),
                 dma((4,)),
+                dma((3, 3, 2, 2)),
                 dma((3, 3, 2)),
-                dma((3, 3)),
+                dma((3, 3, 2, 2)),
                 dma((3, 3, 2)),
-                dma((3, 3)),
+                dma((3, 2, 2)),
                 dma((3, 2)),
-                dma((3, 2)),
-                dma((3, 2)),
+                dma((3, 2, 2)),
                 dma((3, 2)),
                 dma((8,)),
                 dma((8,)),
                 dma((4,)),
                 dma((4,)),
                 dma((8,)),
+                dma((14,)),
+                dma((1,)),
+                pltpu.SemaphoreType.REGULAR((16,)),
             ],
             compiler_params=pltpu.CompilerParams(
                 collective_id=0, has_side_effects=True, vmem_limit_bytes=63 * 2**20

time: 110 us -> 107 us (0.973)
  the two profiles are of different devices: /device:TPU:71 before, /device:TPU:1 now
where the time goes in v3:
time: 107 us; the launch traced here: 106 us
  Pallas kernels  103 us (96%)
  local copies, waits for them, and re-layouts  2.29 us (2%)
  between operations  1.3 us (1%)
    pallas_call x1, Pallas kernels, local(): pl.pallas_call(call, out_shape=jax.ShapeDtypeStruct(queries.shape, BF), i...  103 us
    unnamed x1, local copies, waits for them, and re-layouts  2.29 us

profile of v3, /device:TPU:1, one launch (start us, length us, event | category | flops | bytes accessed | tf_op | source)
XLA Modules:
  0.0 106.2 jit_solution(250589490379196729)
XLA Ops:
  1.3 102.6 %shard_map.82 = bf16[1,128,4096]{2,1,0:T(8,128)(2,1)} custom-call(bf16[1,128,4096]{2,1,0:T(8,128)(2,1)} %args_0_.4, bf16[1,128,4096]{2,1,0:T(8,128)(2,1)} %args_1_.4, bf16[1,128,4096]{2,1,0:T(8,128)(2,1)} %args_2_.4, s32[4]{0:T(128)} %args_3_.4, s32[1]{0:T(128)S(6)} %copy.10.args_4_, s32[1]{0:T(128)S(6)} %copy.11.args_5_, f32[32,128]{1,0:T(8,128)} %bitcast.1, ...), custom_call_target="tpu_custom_call" | custom-call | flops 3288334336 | bytes 8388608 | tf_op jit(solution)/shard_map/pallas_call | solution.py:643
  103.9 2.3 %copy.12 = bf16[1,128,4096]{2,1,0:T(8,128)(2,1)} copy(bf16[1,128,4096]{2,1,0:T(8,128)(2,1)} %shard_map.82) | data formatting | bytes 2097152

commit v4 on v3

--- a/solution.py
+++ b/solution.py
@@ -190,8 +190,7 @@
         src, buf, bx = arrays[a]
 
         def one(tt, carry):
-            below = (8 + z - tt) // 8
-            w = below * (z - tt) + (1 - below) * tt if first else chip_at((tt + 1) % 8)
+            w = chip_at((tt + 1) % 8)
             e = w - 1 - w // 3
             via = (w == (z + 4) % 8) & relayed
 
@@ -642,11 +641,11 @@
         scalars = pl.BlockSpec(memory_space=pltpu.SMEM)
         return pl.pallas_call(
             call,
-            out_shape=jax.ShapeDtypeStruct(queries.shape, BF),
+            out_shape=pltpu.VMEM(queries.shape, BF),
             in_specs=[anywhere] * 3
             + [scalars] * 3
             + [pl.BlockSpec(memory_space=pltpu.VMEM), anywhere],
-            out_specs=anywhere,
+            out_specs=pl.BlockSpec(memory_space=pltpu.VMEM),
             scratch_shapes=[pltpu.VMEM((LIVE, 256), BF)] * 4
             + [pltpu.VMEM((LIVE, HD), BF)] * 4
             + [
@@ -688,7 +687,7 @@
                 pltpu.SemaphoreType.REGULAR((16,)),
             ],
             compiler_params=pltpu.CompilerParams(
-                collective_id=0, has_side_effects=True, vmem_limit_bytes=63 * 2**20
+                collective_id=0, has_side_effects=True, vmem_limit_bytes=62 * 2**20
             ),
             cost_estimate=pl.CostEstimate(
                 flops=4 * 1792 * 1792 * 256,

time: 107 us -> 106 us (level); the launches traced: 106 us -> 104 us
  local copies, waits for them, and re-layouts: 2.29 us -> 0.97 us
    unnamed x1, local copies, waits for them, and re-layouts: 2.29 us -> 0.97 us
where the time goes in v4:
time: 106 us; the launch traced here: 104 us
  Pallas kernels  102 us (96%)
  between operations  1.3 us (1%)
    pallas_call x1, Pallas kernels, local(): pl.pallas_call(call, out_shape=pltpu.VMEM(queries.shape, BF), in_specs=[a...  102 us

profile of v4, /device:TPU:1, one launch (start us, length us, event | category | flops | bytes accessed | tf_op | source)
XLA Modules:
  0.0 104.0 jit_solution(3357899566287047567)
XLA Ops:
  1.3 101.7 %shard_map.82 = bf16[1,128,4096]{2,1,0:T(8,128)(2,1)S(1)} custom-call(bf16[1,128,4096]{2,1,0:T(8,128)(2,1)} %args_0_.4, bf16[1,128,4096]{2,1,0:T(8,128)(2,1)} %args_1_.4, bf16[1,128,4096]{2,1,0:T(8,128)(2,1)} %args_2_.4, s32[4]{0:T(128)} %args_3_.4, s32[1]{0:T(128)S(6)} %copy.11.args_4_, s32[1]{0:T(128)S(6)} %copy.12.args_5_, f32[32,128]{1,0:T(8,128)} %bitcast.1, ...), custom_call_target="tpu_custom_call" | custom-call | flops 3288334336 | bytes 8388608 | tf_op jit(solution)/shard_map/pallas_call | solution.py:642
  103.0 1.0 copy.10

commit v5 on v4

--- a/solution.py
+++ b/solution.py
@@ -109,10 +109,10 @@
     c = i % 2
     y = cl % ny
     x = cl // ny
-    has_x = (c == 0) & (z % 3 != 0) & (i < 14)
+    has_x = (c == 0) & (z % 3 != 1) & (z < 6)
     slot = z // 2
     relayed = (z == 0) | (z == 2) | (z == 5)
-    my_e = z - 1 - z // 3
+    my_e = (z - (z + 1) // 3) % 4
 
     def chip_at(t):
         mag = (4 - t // 2) * ((t + 7) // 8)
@@ -191,7 +191,7 @@
 
         def one(tt, carry):
             w = chip_at((tt + 1) % 8)
-            e = w - 1 - w // 3
+            e = w - (w + 1) // 3
             via = (w == (z + 4) % 8) & relayed
 
             @pl.when(w != 7)
@@ -219,7 +219,7 @@
                     def _():
                         act(rcopy(piece, buf.at[rows_of(i)], ss.at[a, j], rs.at[a, i], j))
 
-                @pl.when(w % 3 != 0)
+                @pl.when((w % 3 != 1) & (w < 6))
                 def _():
                     piece = src.at[0, :, cols(EXTRA0 + 128 * e, 128)]
 
@@ -370,7 +370,7 @@
                     )
                 )
 
-            @pl.when(w % 3 != 0)
+            @pl.when((w % 3 != 1) & (w < 6))
             def _():
                 if wait:
                     arrived(relx.at[a, n, oc], rrx.at[a, n, oc])
@@ -582,7 +582,7 @@
         def forward_result(n, act, wait):
             o = source_of(n)
             w = (o + 4) % 8
-            e = o - 1 - o // 3
+            e = o - (o + 1) // 3
             for cc in (0, 1):
                 for oc in (0, 1):
                     j = 2 * o + oc
@@ -598,7 +598,7 @@
                         )
                     )
 
-                @pl.when(o % 3 != 0)
+                @pl.when((o % 3 != 1) & (o < 6))
                 def _():
                     if wait:
                         arrived(relox.at[n, cc], rrox.at[n, cc])

time: 106 us -> 103 us (0.972)
  Pallas kernels: 102 us -> 99.7 us
    pallas_call x1, Pallas kernels: 102 us -> 99.7 us  [local(): pl.pallas_call(call, out_shape=pltpu.VMEM(queries.shape, BF), in_specs=[a...]
where the time goes in v5:
time: 103 us; the launch traced here: 102 us
  Pallas kernels  99.7 us (97%)
  between operations  1.3 us (1%)
    pallas_call x1, Pallas kernels, local(): pl.pallas_call(call, out_shape=pltpu.VMEM(queries.shape, BF), in_specs=[a...  99.7 us

profile of v5, /device:TPU:1, one launch (start us, length us, event | category | flops | bytes accessed | tf_op | source)
XLA Modules:
  0.0 102.0 jit_solution(13694263900584960977)
XLA Ops:
  1.3 99.7 %shard_map.82 = bf16[1,128,4096]{2,1,0:T(8,128)(2,1)S(1)} custom-call(bf16[1,128,4096]{2,1,0:T(8,128)(2,1)} %args_0_.4, bf16[1,128,4096]{2,1,0:T(8,128)(2,1)} %args_1_.4, bf16[1,128,4096]{2,1,0:T(8,128)(2,1)} %args_2_.4, s32[4]{0:T(128)} %args_3_.4, s32[1]{0:T(128)S(6)} %copy.11.args_4_, s32[1]{0:T(128)S(6)} %copy.12.args_5_, f32[32,128]{1,0:T(8,128)} %bitcast.1, ...), custom_call_target="tpu_custom_call" | custom-call | flops 3288334336 | bytes 8388608 | tf_op jit(solution)/shard_map/pallas_call | solution.py:642
  101.0 1.0 copy.10
